TPU v7x, 128 devices: a whole 4x4x4 slice. The times are simulated.
128 devices in a mesh: replica: 16 (over z, x_lo, core), shard: 8 (over y, x_hi).
Axes of the slice: x: 4 (x_hi: 2, x_lo: 2; x = x_hi * 2 + x_lo), y: 4, z: 4, core: 2. Of those that a mesh axis runs over, the one named last changes fastest.
Arguments:
- images: bfloat16 [768, 197, 384], P(('replica', 'shard')), may hold values from -6 to 6
- cotangent: bfloat16 [768, 197, 384], P(('replica', 'shard')), may hold values from -6 to 6
- image_count: int32 [128], P(('replica', 'shard')), may hold values from 1 to 6, as said below
- joint_weight: float32 [2, 384, 1152], P(None, 'shard'), may hold values from -0.3125 to 0.3125
- merge_weight: float32 [2, 384, 384], P(None, 'shard'), may hold values from -0.625 to 0.625
- expand_weight: float32 [2, 384, 1536], P(None, 'shard'), may hold values from -0.3125 to 0.3125
- reduce_weight: float32 [2, 1536, 384], P(None, 'shard'), may hold values from -0.15625 to 0.15625
- small_params: float32 [2, 3456], P(None, 'shard')
- joint_first: float32 [2, 384, 1152], P(None, 'shard')
- merge_first: float32 [2, 384, 384], P(None, 'shard')
- expand_first: float32 [2, 384, 1536], P(None, 'shard')
- reduce_first: float32 [2, 1536, 384], P(None, 'shard')
- small_first: float32 [2, 3456], P(None, 'shard')
- joint_second: float32 [2, 384, 1152], P(None, 'shard')
- merge_second: float32 [2, 384, 384], P(None, 'shard')
- expand_second: float32 [2, 384, 1536], P(None, 'shard')
- reduce_second: float32 [2, 1536, 384], P(None, 'shard')
- small_second: float32 [2, 3456], P(None, 'shard')
Outputs:
- block_out: float32 [768, 197, 384], P(('replica', 'shard'))
- image_grad: float32 [768, 197, 384], P(('replica', 'shard'))
- joint_grad: float32 [2, 384, 1152], P(None, 'shard')
- merge_grad: float32 [2, 384, 384], P(None, 'shard')
- expand_grad: float32 [2, 384, 1536], P(None, 'shard')
- reduce_grad: float32 [2, 1536, 384], P(None, 'shard')
- small_grad: float32 [2, 3456], P(None, 'shard')
- joint_mean: float32 [2, 384, 1152], P(None, 'shard')
- merge_mean: float32 [2, 384, 384], P(None, 'shard')
- expand_mean: float32 [2, 384, 1536], P(None, 'shard')
- reduce_mean: float32 [2, 1536, 384], P(None, 'shard')
- small_mean: float32 [2, 3456], P(None, 'shard')
- joint_square: float32 [2, 384, 1152], P(None, 'shard')
- merge_square: float32 [2, 384, 384], P(None, 'shard')
- expand_square: float32 [2, 384, 1536], P(None, 'shard')
- reduce_square: float32 [2, 1536, 384], P(None, 'shard')
- small_square: float32 [2, 3456], P(None, 'shard')
- joint_master: float32 [2, 384, 1152], P(None, 'shard')
- merge_master: float32 [2, 384, 384], P(None, 'shard')
- expand_master: float32 [2, 384, 1536], P(None, 'shard')
- reduce_master: float32 [2, 1536, 384], P(None, 'shard')
- small_master: float32 [2, 3456], P(None, 'shard')
Inputs may be any that keep to these rules, and one draw needn't show every extreme that they name: `image_count`: the number of live images among a device's 6 slots; slots from that number on are empty; in every draw some device has 6 and some has 1.
All inputs are finite; a program needn't handle non-finite values.
Results may differ from a plain program's by a relative error of at most 0.015.
The roundings to bfloat16 on the way count: a program that leaves them out, or rounds other values in their place, can miss the bound.
Values may be sent and summed in bfloat16 or wider, within the bound.
A program may use at most 192 MiB of HBM per device.

v0:
```python
import jax
import jax.numpy as jnp
from jax import lax
from jax.sharding import PartitionSpec as P

D = 384
HEADS = 6
HD = 64
LAYERS = 2
STEP = 10


NORM_EPS = 1e-06
BETA_ONE = 0.9
BETA_TWO = 0.999
ADAM_EPS = 1e-08
DECAY_MATRIX = 0.05
RATE_MATRIX = 0.05
RATE_SMALL = 0.4


def side_by_side(arrays, axis, dim, along):
    ends, at = ([], 0)
    for a in arrays[:-1]:
        at += a.shape[along]
        ends.append(at)
    both = jnp.concatenate(arrays, axis=along)
    return tuple(jnp.split(lax.all_gather(both, axis, axis=dim, tiled=True), ends, axis=along))


def layer_norm(inputs, gain_vec, shift_vec):
    centered = inputs - jnp.mean(inputs, axis=-1, keepdims=True)
    variance = jnp.mean(centered * centered, axis=-1, keepdims=True)
    return centered * lax.rsqrt(variance + NORM_EPS) * gain_vec + shift_vec


def exact_gelu(inputs):
    return jax.nn.gelu(inputs, approximate=False)


def split_vector(vector):
    return [vector[position * D : (position + 1) * D] for position in range(5)] + [vector[5 * D :]]


def forward_layer(stream, weights):
    joint, merge, expand, reduce_w, vector = weights
    image_slots, seq_length = (stream.shape[0], stream.shape[1])
    vector_parts = split_vector(vector.astype(jnp.float32))
    normed = layer_norm(stream, vector_parts[0], vector_parts[1]).astype(jnp.bfloat16)
    mixed_rows = jnp.einsum(
        "isd,de->ise", normed, joint, preferred_element_type=jnp.float32
    ).astype(jnp.bfloat16)
    query_rows = mixed_rows[..., :D].reshape(image_slots, seq_length, HEADS, HD)
    key_rows = mixed_rows[..., D : 2 * D].reshape(image_slots, seq_length, HEADS, HD)
    value_rows = mixed_rows[..., 2 * D :].reshape(image_slots, seq_length, HEADS, HD)
    scores = jnp.einsum(
        "iqhe,ikhe->ihqk", query_rows, key_rows, preferred_element_type=jnp.float32
    ) * HD ** (-0.5)
    row_top = jnp.max(scores, axis=-1, keepdims=True)
    exponent = jnp.exp(scores - row_top)
    row_total = jnp.sum(exponent, axis=-1, keepdims=True)
    soft_weights = (exponent / row_total).astype(jnp.bfloat16)
    log_total = row_top + jnp.log(row_total)
    attended = jnp.einsum(
        "ihqk,ikhe->iqhe", soft_weights, value_rows, preferred_element_type=jnp.float32
    )
    attended = attended.astype(jnp.bfloat16).reshape(image_slots, seq_length, D)
    middle = stream + jnp.einsum("isd,de->ise", attended, merge, preferred_element_type=jnp.float32)
    second_normed = layer_norm(middle, vector_parts[2], vector_parts[3]).astype(jnp.bfloat16)
    hidden = (
        jnp.einsum("isd,df->isf", second_normed, expand, preferred_element_type=jnp.float32)
        + vector_parts[5]
    )
    active = exact_gelu(hidden).astype(jnp.bfloat16)
    result = (
        middle
        + jnp.einsum("isf,fd->isd", active, reduce_w, preferred_element_type=jnp.float32)
        + vector_parts[4]
    )
    kept = (
        stream,
        normed,
        query_rows,
        key_rows,
        value_rows,
        log_total,
        attended,
        middle,
        second_normed,
        hidden,
        active,
    )
    return (result, kept)


def backward_layer(grad_out, kept, weights):
    joint, merge, expand, reduce_w, vector = weights
    (
        stream,
        normed,
        query_rows,
        key_rows,
        value_rows,
        log_total,
        attended,
        middle,
        second_normed,
        hidden,
        active,
    ) = kept
    image_slots, seq_length = (stream.shape[0], stream.shape[1])
    vector_parts = split_vector(vector.astype(jnp.float32))
    branch_grad = grad_out.astype(jnp.bfloat16)
    reduce_term = jnp.einsum("isf,isd->fd", active, branch_grad, preferred_element_type=jnp.float32)
    out_bias_term = jnp.sum(branch_grad, axis=(0, 1), dtype=jnp.float32)
    active_grad = jnp.einsum(
        "isd,fd->isf", branch_grad, reduce_w, preferred_element_type=jnp.float32
    )
    hidden_grad = jax.vjp(exact_gelu, hidden)[1](active_grad)[0].astype(jnp.bfloat16)
    expand_term = jnp.einsum(
        "isd,isf->df", second_normed, hidden_grad, preferred_element_type=jnp.float32
    )
    up_bias_term = jnp.sum(hidden_grad, axis=(0, 1), dtype=jnp.float32)
    second_grad = jnp.einsum("isf,df->isd", hidden_grad, expand, preferred_element_type=jnp.float32)
    pullback = jax.vjp(layer_norm, middle, vector_parts[2], vector_parts[3])[1]
    middle_part, gain_two_term, shift_two_term = pullback(second_grad)
    middle_grad = grad_out + middle_part
    merged_grad = middle_grad.astype(jnp.bfloat16)
    merge_term = jnp.einsum(
        "isd,ise->de", attended, merged_grad, preferred_element_type=jnp.float32
    )
    attended_grad = jnp.einsum(
        "ise,de->isd", merged_grad, merge, preferred_element_type=jnp.float32
    )
    attended_grad = attended_grad.astype(jnp.bfloat16).reshape(image_slots, seq_length, HEADS, HD)
    scores = jnp.einsum(
        "iqhe,ikhe->ihqk", query_rows, key_rows, preferred_element_type=jnp.float32
    ) * HD ** (-0.5)
    soft_weights = jnp.exp(scores - log_total)
    value_grad = jnp.einsum(
        "ihqk,iqhe->ikhe",
        soft_weights.astype(jnp.bfloat16),
        attended_grad,
        preferred_element_type=jnp.float32,
    )
    weight_grad = jnp.einsum(
        "iqhe,ikhe->ihqk", attended_grad, value_rows, preferred_element_type=jnp.float32
    )
    score_grad = soft_weights * (
        weight_grad - jnp.sum(weight_grad * soft_weights, axis=-1, keepdims=True)
    )
    score_grad = score_grad.astype(jnp.bfloat16)
    query_grad = jnp.einsum(
        "ihqk,ikhe->iqhe", score_grad, key_rows, preferred_element_type=jnp.float32
    ) * HD ** (-0.5)
    key_grad = jnp.einsum(
        "ihqk,iqhe->ikhe", score_grad, query_rows, preferred_element_type=jnp.float32
    ) * HD ** (-0.5)
    mixed_grad = jnp.concatenate(
        [
            query_grad.reshape(image_slots, seq_length, D),
            key_grad.reshape(image_slots, seq_length, D),
            value_grad.reshape(image_slots, seq_length, D),
        ],
        axis=-1,
    ).astype(jnp.bfloat16)
    joint_term = jnp.einsum("isd,ise->de", normed, mixed_grad, preferred_element_type=jnp.float32)
    normed_grad = jnp.einsum("ise,de->isd", mixed_grad, joint, preferred_element_type=jnp.float32)
    pullback = jax.vjp(layer_norm, stream, vector_parts[0], vector_parts[1])[1]
    stream_part, gain_one_term, shift_one_term = pullback(normed_grad)
    small_term = jnp.concatenate(
        [gain_one_term, shift_one_term, gain_two_term, shift_two_term, out_bias_term, up_bias_term]
    )
    return (
        middle_grad + stream_part,
        (joint_term, merge_term, expand_term, reduce_term, small_term),
    )


def adam_update(gradient, first_moment, second_moment, master, step_rate, decay_rate):
    first_new = BETA_ONE * first_moment + (1.0 - BETA_ONE) * gradient
    second_new = BETA_TWO * second_moment + (1.0 - BETA_TWO) * gradient * gradient
    corrected = first_new / (1.0 - BETA_ONE**STEP)
    denominator = jnp.sqrt(second_new / (1.0 - BETA_TWO**STEP)) + ADAM_EPS
    master_new = master - step_rate * (corrected / denominator + decay_rate * master)
    return (first_new, second_new, master_new)


def regroup(gradient, n_shard, n_replica):
    full_shape = gradient.shape
    piece_width = full_shape[1] // (n_shard * n_replica)
    split_view = gradient.reshape(
        full_shape[:1] + (n_shard, n_replica, piece_width) + full_shape[2:]
    )
    return jnp.swapaxes(split_view, 1, 2).reshape(full_shape)


def shards(
    images,
    cotangent,
    image_count,
    joint_weight,
    merge_weight,
    expand_weight,
    reduce_weight,
    small_params,
    joint_first,
    merge_first,
    expand_first,
    reduce_first,
    small_first,
    joint_second,
    merge_second,
    expand_second,
    reduce_second,
    small_second,
):
    masters = (joint_weight, merge_weight, expand_weight, reduce_weight, small_params)
    firsts = (joint_first, merge_first, expand_first, reduce_first, small_first)
    seconds = (joint_second, merge_second, expand_second, reduce_second, small_second)
    step_rates = (RATE_MATRIX, RATE_MATRIX, RATE_MATRIX, RATE_MATRIX, RATE_SMALL)
    decay_rates = (DECAY_MATRIX, DECAY_MATRIX, DECAY_MATRIX, DECAY_MATRIX, 0.0)
    live_mask = (jnp.arange(images.shape[0]) < image_count[0]).astype(jnp.float32)[:, None, None]
    low_copy = [member.astype(jnp.bfloat16) for member in masters]
    fetched = (
        *side_by_side((low_copy[0], low_copy[1], low_copy[2]), "shard", 1, 2),
        lax.all_gather(low_copy[3], "shard", axis=1, tiled=True),
        lax.all_gather(low_copy[4], "shard", axis=1, tiled=True),
    )
    stream = images.astype(jnp.float32)
    stored = []
    for layer_index in range(LAYERS):
        stream, kept = forward_layer(stream, tuple((member[layer_index] for member in fetched)))
        stored.append(kept)
    block_out = stream * live_mask
    gradient = cotangent.astype(jnp.float32) * live_mask
    layer_terms = [None] * LAYERS
    for layer_index in reversed(range(LAYERS)):
        gradient, layer_terms[layer_index] = backward_layer(
            gradient, stored[layer_index], tuple((member[layer_index] for member in fetched))
        )
    local_sums = [
        jnp.stack([layer_terms[layer_index][kind_index] for layer_index in range(LAYERS)])
        for kind_index in range(5)
    ]
    n_shard = lax.axis_size("shard")
    n_replica = lax.axis_size("replica")
    ordered = [regroup(member, n_shard, n_replica) for member in local_sums]
    pieces = (
        lax.psum_scatter(ordered[0], ("replica", "shard"), scatter_dimension=1, tiled=True),
        lax.psum_scatter(ordered[1], ("replica", "shard"), scatter_dimension=1, tiled=True),
        lax.psum_scatter(ordered[2], ("replica", "shard"), scatter_dimension=1, tiled=True),
        lax.psum_scatter(ordered[3], ("replica", "shard"), scatter_dimension=1, tiled=True),
        lax.psum_scatter(ordered[4], ("replica", "shard"), scatter_dimension=1, tiled=True),
    )
    replica_rank = lax.axis_index("replica")
    shares = []
    for kind_index in range(5):
        piece_width = pieces[kind_index].shape[1]
        offset_start = replica_rank * piece_width
        owned = [
            lax.dynamic_slice_in_dim(member, offset_start, piece_width, 1)
            for member in (firsts[kind_index], seconds[kind_index], masters[kind_index])
        ]
        updated = adam_update(
            pieces[kind_index],
            owned[0],
            owned[1],
            owned[2],
            step_rates[kind_index],
            decay_rates[kind_index],
        )
        shares.append((pieces[kind_index],) + updated)
    returned = (
        *side_by_side(
            (
                shares[0][0],
                shares[0][1],
                shares[0][2],
                shares[0][3],
                shares[1][0],
                shares[1][1],
                shares[1][2],
                shares[1][3],
                shares[2][0],
                shares[2][1],
                shares[2][2],
                shares[2][3],
            ),
            "replica",
            1,
            2,
        ),
        *side_by_side((shares[3][0], shares[3][1], shares[3][2], shares[3][3]), "replica", 1, 0),
        *side_by_side((shares[4][0], shares[4][1], shares[4][2], shares[4][3]), "replica", 1, 0),
    )
    results = [
        tuple((returned[4 * kind_index + member_index] for member_index in range(4)))
        for kind_index in range(5)
    ]
    outputs = [block_out, gradient]
    for member_index in range(4):
        outputs = outputs + [results[kind_index][member_index] for kind_index in range(5)]
    return tuple(outputs)


def solution(mesh):
    placed = (
        P(("replica", "shard"), None, None),
        P(("replica", "shard"), None, None),
        P(("replica", "shard")),
        P(None, "shard", None),
        P(None, "shard", None),
        P(None, "shard", None),
        P(None, "shard", None),
        P(None, "shard"),
        P(None, "shard", None),
        P(None, "shard", None),
        P(None, "shard", None),
        P(None, "shard", None),
        P(None, "shard"),
        P(None, "shard", None),
        P(None, "shard", None),
        P(None, "shard", None),
        P(None, "shard", None),
        P(None, "shard"),
    )
    return jax.shard_map(
        shards,
        mesh=mesh,
        in_specs=placed,
        out_specs=(
            P(("replica", "shard"), None, None),
            P(("replica", "shard"), None, None),
            P(None, "shard", None),
            P(None, "shard", None),
            P(None, "shard", None),
            P(None, "shard", None),
            P(None, "shard"),
            P(None, "shard", None),
            P(None, "shard", None),
            P(None, "shard", None),
            P(None, "shard", None),
            P(None, "shard"),
            P(None, "shard", None),
            P(None, "shard", None),
            P(None, "shard", None),
            P(None, "shard", None),
            P(None, "shard"),
            P(None, "shard", None),
            P(None, "shard", None),
            P(None, "shard", None),
            P(None, "shard", None),
            P(None, "shard"),
        ),
        check_vma=False,
    )
```

profile of v0, /device:TPU:1, one launch (start us, length us, event | category | flops | bytes accessed | tf_op | source)
XLA Modules:
  0.0 689.2 jit_solution(17358650884970678098)
XLA Ops:
  12.2 26.7 %all-gather = bf16[8,432,2]{1,2,0:T(2,128)(2,1)S(1)} all-gather(bf16[1,432,2]{1,2,0:T(2,128)(2,1)S(1)} %convert_bitcast_fusion), channel_id=1, replica_groups=mesh['replica'=16,'shard'=8] {'shard'}, dimensions={0}, use_global_device_ids=true | all-gather | bytes 15552 | tf_op jit(solution)/shard_map/all_gather | solution.py:228
  41.4 48.7 %all-gather.7.cloned.1.call-done = bf16[2,384,3072]{2,1,0:T(8,128)(2,1)} async-done(((bf16[2,48,3072]{2,1,0:T(8,128)(2,1)}), bf16[2,384,3072]{2,1,0:T(8,128)(2,1)}) %all-gather.7.cloned.1.call-update) | async-done | bytes 4718608 | tf_op jit(solution)/shard_map/all_gather | solution.py:28
  90.1 3.1 convolution_convert_fusion.1
  97.8 2.7 copy.258
  100.5 2.5 multiply_reduce_fusion.3
  110.5 5.3 fusion.40
  115.8 2.9 copy-done.28
  118.7 18.0 %multiply_convert_fusion.3 = (bf16[6,197,1536]{2,1,0:T(8,128)(2,1)}, f32[6,197,1536]{2,1,0:T(8,128)}) fusion(f32[6,197,1536]{2,1,0:T(8,128)S(1)} %get-tuple-element.194, f32[1536]{0:T(1024)S(1)} %get-tuple-element.215, u8[197,1536]{1,0:T(8,128)(4,1)S(1)} %get-tuple-element.113, u8[197,1536]{1,0:T(8,128)(4,1)S(1)} %get-tuple-element.112), kind=kLoop, calls=%fused_computation.38 | loop fusion | flops 128904192 | bytes 18766848 | tf_op jit(solution)/shard_map/convert_element_type | solution.py:74
  136.7 10.1 %all-gather.9.cloned.1.call-done = bf16[2,1536,384]{2,1,0:T(8,128)(2,1)} async-done(((bf16[2,192,384]{2,1,0:T(8,128)(2,1)}), bf16[2,1536,384]{2,1,0:T(8,128)(2,1)}) %all-gather.9.cloned.1.call-update) | async-done | bytes 2359312 | tf_op jit(solution)/shard_map/all_gather | solution.py:227
  146.8 4.6 fusion.112
  152.0 3.2 convolution_convert_fusion
  165.4 5.3 fusion.48
  170.7 2.2 fusion.113
  173.4 5.2 fusion.41
  178.6 17.6 %multiply_convert_fusion.2 = (bf16[6,197,1536]{2,1,0:T(8,128)(2,1)}, f32[6,197,1536]{2,1,0:T(8,128)S(1)}) fusion(f32[6,197,1536]{2,1,0:T(8,128)S(1)} %get-tuple-element.201, f32[1536]{0:T(1024)S(1)} %get-tuple-element.214, u8[197,1536]{1,0:T(8,128)(4,1)S(1)} %get-tuple-element.111, u8[197,1536]{1,0:T(8,128)(4,1)S(1)} %get-tuple-element.110), kind=kLoop, calls=%fused_computation.23 | loop fusion | flops 128904192 | bytes 18766848 | tf_op jit(solution)/shard_map/convert_element_type | solution.py:74
  196.2 5.2 convert_reduce_fusion
  201.5 4.7 multiply_reduce_fusion.4
  209.9 2.8 convolution_convert_fusion.3
  212.7 2.3 copy.268
  215.1 6.0 multiply_reduce_fusion.1
  224.8 2.3 multiply_convert_fusion.6
  227.1 2.5 fusion.42
  231.0 2.4 copy.273
  233.4 2.3 copy.274
  235.8 4.5 fusion.95
  243.6 8.1 %convert_reduce_fusion.1 = (f32[1536]{0:T(1024)S(1)}, bf16[6,197,1536]{2,1,0:T(8,128)(2,1)S(1)}) fusion(f32[6,197,1536]{2,1,0:T(8,128)} %get-tuple-element.159, bf16[2,1536,384]{2,1,0:T(8,128)(2,1)S(1)} %copy-done.64, f32[6,197,384]{2,1,0:T(8,128)S(1)} %get-tuple-element.147, f32[6,197,1536]{2,1,0:T(8,128)} %copy-done.28, f32[1536]{0:T(1024)S(1)} %get-tuple-element.215), kind=kOutput, calls=%fused_computation.14 | convolution fusion | flops 1425660672 | bytes 21192704 | tf_op jit(solution)/shard_map/isd,fd->isf/dot_general | solution.py:116
  251.7 4.8 multiply_reduce_fusion.6
  261.1 2.7 convolution_convert_fusion.2
  265.3 5.6 multiply_reduce_fusion
  271.0 2.2 multiply_convert_fusion
  275.1 2.4 multiply_convert_fusion.4
  277.4 2.5 fusion.45
  280.4 3.7 convolution_bitcast_fusion.3
  284.1 3.4 convolution_bitcast_fusion.5
  287.5 3.3 convolution_bitcast_fusion.4
  290.8 3.1 convolution_bitcast_fusion
  295.2 2.3 copy.280
  297.5 2.4 copy.281
  300.0 3.7 stack.48
  303.6 5.8 convolution_bitcast_fusion.2
  309.4 3.8 stack.49
  313.3 3.3 maximum_bitcast_fusion.1
  316.6 5.8 copy.296
  322.3 4.4 stack.45
  326.8 4.5 stack.46
  331.3 4.5 maximum_bitcast_fusion
  335.8 5.8 copy.292
  341.6 3.9 reshape.341
  345.5 3.2 convolution_bitcast_fusion.6
  348.7 2.2 reshape.340
  351.0 2.5 convolution_bitcast_fusion.7
  356.6 3.1 convolution_bitcast_fusion.1
  359.7 3.8 stack.41
  363.5 3.8 stack.42
  367.3 3.6 maximum_bitcast_fusion.2
  370.9 4.6 copy.282
  380.1 166.2 %all-reduce.8.cloned.1.call-done = (f32[2,384,1152]{2,0,1:T(2,128)}, f32[2,384,384]{2,0,1:T(2,128)}, f32[2,384,1536]{2,0,1:T(2,128)}, f32[2,1536,384]{2,0,1:T(2,128)}) async-done(((f32[2,384,1152]{2,0,1:T(2,128)}, f32[2,384,384]{2,0,1:T(2,128)}, f32[2,384,1536]{2,0,1:T(2,128)}, f32[2,1536,384]{2,0,1:T(2,128)}), (f32[2,384,1152]{2,0,1:T(2,128)}, f32[2,384,384]{2,0,1:T(2,128)}, f32[2,384,1536]{2,0,1:T(2,128)}, ...) | async-done | bytes 14155792
  561.1 3.9 fusion.94
  568.2 64.9 %all-reduce.4 = f32[2,3456]{1,0:T(2,128)S(1)} all-reduce(f32[2,3456]{1,0:T(2,128)S(1)} %reshape.345), channel_id=6, replica_groups=mesh['replica'=16,'shard'=8] {'replica','shard'}, use_global_device_ids=true, to_apply=%region_38.0.clone | all-reduce | flops 6912 | bytes 55296
  633.9 18.3 %all-gather.1 = f32[16,27,8]{1,2,0:T(8,128)S(1)} all-gather(f32[1,27,8]{1,2,0:T(8,128)S(1)} %maximum_bitcast_fusion.5), channel_id=1, replica_groups=mesh['replica'=16,'shard'=8] {'replica'}, dimensions={0}, use_global_device_ids=true | all-gather | bytes 14688 | tf_op jit(solution)/shard_map/all_gather | solution.py:28
  652.9 4.1 add_add_fusion.4
  658.0 3.3 add_multiply_fusion
  661.3 4.9 fusion.109
  669.7 2.4 fusion.104
  (279 shorter events, 93.4 us)
Async XLA Ops:
  7.2 4.2 copy-start.49
  7.2 5.0 copy-start.59
  7.2 32.5 %copy-start.9 = (bf16[6,197,384]{2,1,0:T(8,128)(2,1)S(1)}, bf16[6,197,384]{2,1,0:T(8,128)(2,1)}, u32[]{:S(2)}) copy-start(bf16[6,197,384]{2,1,0:T(8,128)(2,1)} %param.18) | copy-start | bytes 2723332
  7.2 82.8 %all-gather.7.cloned.1.call-start = ((), (), s32[]{:S(2)}) async-start(), calls=%async_computation | async-start | bytes 5308416 | tf_op jit(solution)/shard_map/all_gather | solution.py:28
  11.3 135.5 %all-gather.9.cloned.1.call-start = ((), (), s32[]{:S(2)}) async-start(), calls=%async_computation.1 | async-start | bytes 2654208 | tf_op jit(solution)/shard_map/all_gather | solution.py:227
  12.2 534.1 %all-reduce.8.cloned.1.call-start = ((), (), s32[]{:S(2)}) async-start(), calls=%async_computation.4 | async-start | bytes 28311552
  39.7 53.5 %copy-start.57 = (f32[384]{0:T(512)}, f32[384]{0:T(512)S(1)}, u32[]{:S(2)}) copy-start(f32[384]{0:T(512)S(1)} %get-tuple-element.216) | copy-start | bytes 4612
  39.7 53.5 %copy-start.61 = (f32[384]{0:T(512)}, f32[384]{0:T(512)S(1)}, u32[]{:S(2)}) copy-start(f32[384]{0:T(512)S(1)} %get-tuple-element.217) | copy-start | bytes 4612
  40.0 50.0 %copy-start.51 = (f32[6,197]{1,0:T(8,128)}, f32[6,197]{1,0:T(8,128)S(1)}, u32[]{:S(2)}) copy-start(f32[6,197]{1,0:T(8,128)S(1)} %broadcast_multiply_fusion.3) | copy-start | bytes 14188
  40.7 49.4 %copy-start.55 = (f32[6,197]{1,0:T(8,128)}, f32[6,197]{1,0:T(8,128)S(1)}, u32[]{:S(2)}) copy-start(f32[6,197]{1,0:T(8,128)S(1)} %fusion.35) | copy-start | bytes 14188
  40.7 49.4 %copy-start.53 = (f32[6,197]{1,0:T(8,128)}, f32[6,197]{1,0:T(8,128)S(1)}, u32[]{:S(2)}) copy-start(f32[6,197]{1,0:T(8,128)S(1)} %fusion.74) | copy-start | bytes 14188
  97.8 5.2 copy-start.15
  103.0 3.0 copy-start
  103.1 3.0 copy-start.29
  107.8 2.7 copy-start.32
  109.9 36.9 %copy-start.2 = (f32[6,197,384]{2,1,0:T(8,128)}, f32[6,197,384]{2,1,0:T(8,128)S(1)}, u32[]{:S(2)}) copy-start(f32[6,197,384]{2,1,0:T(8,128)S(1)} %get-tuple-element.193) | copy-start | bytes 5446660
  115.8 2.9 copy-start.28
  151.5 3.7 copy-start.5
  157.3 3.1 copy-start.19
  160.4 3.0 copy-start.1
  165.3 5.3 copy-start.30
  165.4 5.3 copy-start.6
  170.7 7.9 %copy-start.34 = (bf16[6,6,64,197]{3,2,1,0:T(8,128)(2,1)}, bf16[6,6,64,197]{3,2,1,0:T(8,128)(2,1)S(1)}, u32[]{:S(2)}) copy-start(bf16[6,6,64,197]{3,2,1,0:T(8,128)(2,1)S(1)} %fusion.48) | copy-start | bytes 2723332
  178.6 17.6 %copy-start.38 = (bf16[6,197,384]{2,1,0:T(8,128)(2,1)S(1)}, bf16[6,197,384]{2,1,0:T(8,128)(2,1)}, u32[]{:S(2)}) copy-start(bf16[6,197,384]{2,1,0:T(8,128)(2,1)} %param.19) | copy-start | bytes 2723332
  178.6 17.6 %copy-start.63 = (bf16[2,1536,384]{2,1,0:T(8,128)(2,1)S(1)}, bf16[2,1536,384]{2,1,0:T(8,128)(2,1)}, u32[]{:S(2)}) copy-start(bf16[2,1536,384]{2,1,0:T(8,128)(2,1)} %all-gather.9.cloned.1.call-done) | copy-start | bytes 7077892
  201.5 4.7 copy-start.21
  215.1 6.0 slice-start.2
  215.1 6.0 slice-start.3
  224.8 2.3 copy-start.17
  227.1 2.5 copy-start.26
  231.0 4.7 copy-start.45
  235.8 4.5 copy-start.7
  243.1 15.2 %copy-start.11 = (f32[6,197,384]{2,1,0:T(8,128)}, f32[6,197,384]{2,1,0:T(8,128)S(1)}, u32[]{:S(2)}) copy-start(f32[6,197,384]{2,1,0:T(8,128)S(1)} %get-tuple-element.147) | copy-start | bytes 5446660
  243.6 8.1 %copy-start.3 = (f32[6,197,384]{2,1,0:T(8,128)S(1)}, f32[6,197,384]{2,1,0:T(8,128)}, u32[]{:S(2)}) copy-start(f32[6,197,384]{2,1,0:T(8,128)} %copy-done.2) | copy-start | bytes 5446660
  251.7 4.9 copy-start.23
  265.3 5.7 slice-start
  265.3 5.7 slice-start.1
  277.4 2.5 copy-start.12
  277.4 2.9 copy-start.36
  280.4 3.7 copy-start.4
  280.4 3.7 copy-start.24
  284.1 3.4 copy-start.22
  287.5 3.3 copy-start.8
  287.5 3.3 copy-start.46
  287.5 3.3 copy-start.47
  287.5 3.3 copy-start.48
  290.8 3.1 copy-start.25
  297.5 6.1 copy-start.40
  341.6 7.1 %copy-start.33 = (bf16[6,6,64,197]{3,2,1,0:T(8,128)(2,1)S(1)}, bf16[6,6,64,197]{3,2,1,0:T(8,128)(2,1)}, u32[]{:S(2)}) copy-start(bf16[6,6,64,197]{3,2,1,0:T(8,128)(2,1)} %copy-done.32) | copy-start | bytes 2723332
  350.9 5.7 copy-start.10
  350.9 5.7 copy-start.42
  350.9 5.7 copy-start.43
  350.9 5.7 copy-start.44
  350.9 5.7 copy-start.52
  350.9 5.7 copy-start.54
  350.9 5.7 copy-start.58
  350.9 5.7 copy-start.62
  375.5 285.9 %all-gather.13.cloned.1.call-start = ((), (), s32[]{:S(2)}) async-start(), calls=%async_computation.3 | async-start | bytes 2506752 | tf_op jit(solution)/shard_map/all_gather | solution.py:28
  548.0 121.7 %all-gather.11.cloned.1.call-start = ((), (), s32[]{:S(2)}) async-start(), calls=%async_computation.2 | async-start | bytes 5013504 | tf_op jit(solution)/shard_map/all_gather | solution.py:28
  561.1 3.9 copy-start.56
  652.9 4.2 copy-start.35
  652.9 4.2 copy-start.60
  652.9 5.1 copy-start.65
  672.1 3.7 copy-start.31
  (11 other events, 15.9 us)
Sparse Core Ops, SparseCore 0:
  11.5 78.5 all-gather.6
  93.0 53.8 all-gather.8
  375.6 170.6 all-reduce.7
  548.5 33.0 all-gather.12
  583.9 38.7 all-gather.10
where the time goes:
time: 695 us; the launch traced here: 689 us
  waiting for transfers between devices  225 us (32%)
  matrix products  130 us (19%)
  local copies, waits for them, and re-layouts  124 us (18%)
  blocking collectives  110 us (16%)
  other arithmetic  84.7 us (12%)
  between operations  16 us (2%)
    unnamed x6, waiting for transfers between devices  166 us
    unnamed x1, blocking collectives  64.9 us
    all_gather x3, waiting for transfers between devices, side_by_side(): lax.all_gather(both, axis, axis=dim, tiled=True)  48.7 us
    convert_element_type x2, other arithmetic, forward_layer(): active = exact_gelu(hidden).astype(jnp.bfloat16)  35.6 us
    unnamed x171, local copies, waits for them, and re-layouts  29 us
    all_gather x1, blocking collectives, shards(): lax.all_gather(low_copy[4], 'shard', axis=1, tiled=True)  26.7 us
    another operation x8, local copies, waits for them, and re-layouts, shards(): jnp.stack([layer_terms[layer_index][kind_index] for layer_index in range(...  24.5 us
    all_gather x1, blocking collectives, side_by_side(): lax.all_gather(both, axis, axis=dim, tiled=True)  18.3 us
  transfers between devices with their start and end apart: 5, of which 3 were waited for; matrix products, arithmetic and copies ran while one was open for 12% of the time, Pallas kernels for 0%

commit v1 on v0

v1 whole, which is shorter than its diff:
```python
import jax
import jax.numpy as jnp
from jax import lax
from jax.experimental import pallas as pl
from jax.experimental.pallas import tpu as pltpu
from jax.sharding import PartitionSpec as P

D = 384
FF = 1536
BLK = 640
F32 = jnp.float32
BF16 = jnp.bfloat16
HD = 64
NI = 6
SEQ = 197
R = 208
T = NI * R
CH = 416
NCH = T // CH
NORM_EPS = 1e-6


def dot(a, b):
    return lax.dot_general(a, b, (((1,), (0,)), ((), ())), preferred_element_type=F32)


def dot_nt(a, b):
    return lax.dot_general(a, b, (((1,), (1,)), ((), ())), preferred_element_type=F32)


def dot_tn(a, b):
    return lax.dot_general(a, b, (((0,), (0,)), ((), ())), preferred_element_type=F32)


def normalize(v):
    centered = v - jnp.mean(v, axis=-1, keepdims=True)
    variance = jnp.mean(centered * centered, axis=-1, keepdims=True)
    rstd = lax.rsqrt(variance + NORM_EPS)
    return centered * rstd, rstd


def gelu_pair(u):
    z = jnp.abs(u)
    d = 1.0 + (0.3275911 * 0.7071067811865476) * z
    t = 1.0 / d
    e = jnp.exp(-0.5 * (u * u))
    poly = ((((0.5 * 1.061405429) * t - 0.5 * 1.453152027) * t + 0.5 * 1.421413741) * t
            - 0.5 * 0.284496736) * t + 0.5 * 0.254829592
    half = poly * t * e
    phi = jnp.where(u < 0, half, 1.0 - half)
    return u * phi, phi + u * (e * 0.3989422804014327)


def norm_back(dy, xhat, rstd, gain):
    dxh = dy * gain
    m1 = jnp.mean(dxh, axis=-1, keepdims=True)
    m2 = jnp.mean(dxh * xhat, axis=-1, keepdims=True)
    return rstd * (dxh - m1 - xhat * m2)


def compute_kernel(count, img, cot, w_all, sp, out, dimg, g_all,
                   wj, wm, we, wr, xs, hs, a_s, c_s, o_s, qkv, g_s, gp_s, dx_s, dzb_s, dyb_s,
                   dob_s, lse_s, grad, small, wsem, gsem):
    def rows_of(c):
        return pl.ds(pl.multiple_of(c * CH, CH), CH)

    def img_rows(i, n=R):
        return pl.ds(pl.multiple_of(i * R, R), n)

    def weight_copies(l):
        out_list = []
        for cb in range(3):
            out_list.append((w_all.at[l, :, pl.ds(48 * cb, 48), :],
                             wj.at[l, :, :, pl.ds(D * cb, D)], 0))
        out_list.append((w_all.at[l, :, pl.ds(144, 48), :], wm.at[l], 1))
        for cb in range(4):
            out_list.append((w_all.at[l, :, pl.ds(192 + 48 * cb, 48), :],
                             we.at[l, :, :, pl.ds(D * cb, D)], 2))
        out_list.append((w_all.at[l, :, pl.ds(384, 192), :], wr.at[l], 3))
        return [pltpu.make_async_copy(s, d, wsem.at[l, k]) for k, (s, d, _) in enumerate(out_list)]

    copies = [weight_copies(0), weight_copies(1)]
    for l in range(2):
        for cp in copies[l]:
            cp.start()

    n_live = count[0]

    def load(i, _):
        live = jnp.where(i < n_live, 1.0, 0.0).astype(F32)
        tail = pl.ds(pl.multiple_of(i * R, R) + 192, 16)
        xs[0, tail, :] = jnp.zeros((16, D), F32)
        dx_s[tail, :] = jnp.zeros((16, D), F32)
        xs[0, img_rows(i, SEQ), :] = img[i].astype(F32)
        dx_s[img_rows(i, SEQ), :] = cot[i].astype(F32) * live
        return 0

    lax.fori_loop(0, NI, load, 0)

    lane = lax.broadcasted_iota(jnp.int32, (R, 128), 1)
    key_ok = lax.broadcasted_iota(jnp.int32, (R, R), 0) < SEQ

    def half(v, e):
        keep = (lane < HD) if e == 0 else (lane >= HD)
        return jnp.where(keep, v, jnp.zeros_like(v))

    for l in range(2):
        vec = lambda r: sp[l, r:r + 1, :]
        for cp in copies[l][:3]:
            cp.wait()

        def p1(c, _):
            rows = rows_of(c)
            xhat, _r = normalize(xs[l, rows, :])
            a = (xhat * vec(0) + vec(1)).astype(BF16)
            a_s[l, rows, :] = a
            for cb in range(3):
                part = dot(a, wj[l, :, :, pl.ds(D * cb, D)].reshape(D, D))
                if cb == 0:
                    part = part * (HD ** -0.5)
                qkv[l, rows, pl.ds(D * cb, D)] = part.astype(BF16)
            return 0

        lax.fori_loop(0, NCH, p1, 0)

        def p2(i, _):
            rows = img_rows(i)
            for j in range(3):
                q2 = qkv[l, rows, pl.ds(128 * j, 128)]
                k2 = qkv[l, rows, pl.ds(D + 128 * j, 128)]
                v2 = qkv[l, rows, pl.ds(2 * D + 128 * j, 128)]
                v2t = v2.T
                parts = []
                for e in range(2):
                    st = dot_nt(k2, half(q2, e))
                    st = jnp.where(key_ok, st, -1e30)
                    m = jnp.max(st, axis=0, keepdims=True)
                    pt = jnp.exp(st - m)
                    tot = jnp.sum(pt, axis=0, keepdims=True)
                    pbt = (pt * (1.0 / tot)).astype(BF16)
                    lse_s[l, i, 2 * j + e:2 * j + e + 1, :] = m + jnp.log(tot)
                    parts.append(dot(v2t[HD * e:HD * (e + 1), :], pbt))
                o_s[l, rows, pl.ds(128 * j, 128)] = jnp.concatenate(parts, axis=0).T.astype(BF16)
            return 0

        lax.fori_loop(0, NI, p2, 0)

        for cp in copies[l][3:]:
            cp.wait()

        def p3(c, _):
            rows = rows_of(c)
            h = xs[l, rows, :] + dot(o_s[l, rows, :], wm[l].reshape(D, D))
            hs[l, rows, :] = h
            xhat, _r = normalize(h)
            cc = (xhat * vec(2) + vec(3)).astype(BF16)
            c_s[l, rows, :] = cc
            acc = h + vec(4)
            for f in range(4):
                u = dot(cc, we[l, :, :, pl.ds(D * f, D)].reshape(D, D)) + vec(5 + f)
                g, gp = gelu_pair(u)
                g = g.astype(BF16)
                g_s[l, rows, pl.ds(D * f, D)] = g
                gp_s[l, rows, pl.ds(D * f, D)] = gp.astype(BF16)
                acc = acc + dot(g, wr[l, 2 * f:2 * f + 2].reshape(D, D))
            if l == 0:
                xs[1, rows, :] = acc
            else:
                for k in range(CH // R):
                    i = c * (CH // R) + k
                    live = jnp.where(i < n_live, 1.0, 0.0).astype(F32)
                    out[i] = acc[R * k:R * k + SEQ, :] * live
            return 0

        lax.fori_loop(0, NCH, p3, 0)

    small[...] = jnp.zeros_like(small)

    def colsum(v):
        return jnp.sum(v, axis=0, keepdims=True)

    for l in (1, 0):
        vec = lambda r: sp[l, r:r + 1, :]

        def b1(c, _):
            rows = rows_of(c)
            dx = dx_s[rows, :]
            dzb = dx.astype(BF16)
            dzb_s[rows, :] = dzb
            small[l, 4:5, :] += colsum(dzb.astype(F32))
            dc = None
            for f in range(4):
                dg = dot_nt(dzb, wr[l, 2 * f:2 * f + 2].reshape(D, D))
                du = (dg * gp_s[l, rows, pl.ds(D * f, D)].astype(F32)).astype(BF16)
                gp_s[l, rows, pl.ds(D * f, D)] = du
                small[l, 5 + f:6 + f, :] += colsum(du.astype(F32))
                part = dot_nt(du, we[l, :, :, pl.ds(D * f, D)].reshape(D, D))
                dc = part if dc is None else dc + part
            xhat, rstd = normalize(hs[l, rows, :])
            small[l, 2:3, :] += colsum(dc * xhat)
            small[l, 3:4, :] += colsum(dc)
            dh = dx + norm_back(dc, xhat, rstd, vec(2))
            dx_s[rows, :] = dh
            dyb = dh.astype(BF16)
            dyb_s[rows, :] = dyb
            dob_s[rows, :] = dot_nt(dyb, wm[l].reshape(D, D)).astype(BF16)
            return 0

        lax.fori_loop(0, NCH, b1, 0)

        def b2(i, _):
            rows = img_rows(i)
            for j in range(3):
                q2 = qkv[l, rows, pl.ds(128 * j, 128)]
                k2 = qkv[l, rows, pl.ds(D + 128 * j, 128)]
                v2 = qkv[l, rows, pl.ds(2 * D + 128 * j, 128)]
                do2 = dob_s[rows, pl.ds(128 * j, 128)]
                k2t = k2.T
                dv = dk = None
                dqt = []
                for e in range(2):
                    qe = half(q2, e)
                    de = half(do2, e)
                    st = dot_nt(k2, qe)
                    pt = jnp.where(key_ok, jnp.exp(st - lse_s[l, i, 2 * j + e:2 * j + e + 1, :]), 0.0)
                    dpt = dot_nt(v2, de)
                    r = jnp.sum(dpt * pt, axis=0, keepdims=True)
                    dst = (pt * (dpt - r)).astype(BF16)
                    dve = dot(pt.astype(BF16), de)
                    dke = dot(dst, qe)
                    dv = dve if dv is None else dv + dve
                    dk = dke if dk is None else dk + dke
                    dqt.append(dot(k2t[HD * e:HD * (e + 1), :], dst))
                dq = jnp.concatenate(dqt, axis=0).T * (HD ** -0.5)
                qkv[l, rows, pl.ds(128 * j, 128)] = dq.astype(BF16)
                qkv[l, rows, pl.ds(D + 128 * j, 128)] = dk.astype(BF16)
                qkv[l, rows, pl.ds(2 * D + 128 * j, 128)] = dv.astype(BF16)
            return 0

        lax.fori_loop(0, NI, b2, 0)

        def b3(c, _):
            rows = rows_of(c)
            da = None
            for cb in range(3):
                part = dot_nt(qkv[l, rows, pl.ds(D * cb, D)],
                              wj[l, :, :, pl.ds(D * cb, D)].reshape(D, D))
                da = part if da is None else da + part
            xhat, rstd = normalize(xs[l, rows, :])
            small[l, 0:1, :] += colsum(da * xhat)
            small[l, 1:2, :] += colsum(da)
            dx = dx_s[rows, :] + norm_back(da, xhat, rstd, vec(0))
            if l == 1:
                dx_s[rows, :] = dx
            else:
                for k in range(CH // R):
                    dimg[c * (CH // R) + k] = dx[R * k:R * k + SEQ, :]
            return 0

        lax.fori_loop(0, NCH, b3, 0)

        def shard_store(at, rows, val):
            grad[l, :, pl.ds(at, rows), :] = val.astype(BF16).reshape(8, rows, D)

        for cb in range(3):
            shard_store(48 * cb, 48, dot_tn(a_s[l], qkv[l, :, pl.ds(D * cb, D)]))
        shard_store(144, 48, dot_tn(o_s[l], dyb_s[...]))
        for f in range(4):
            shard_store(192 + 48 * f, 48, dot_tn(c_s[l], gp_s[l, :, pl.ds(D * f, D)]))
        for f in range(4):
            val = dot_tn(dzb_s[...], g_s[l, :, pl.ds(D * f, D)])
            grad[l, 2 * f:2 * f + 2, pl.ds(384, 192), :] = val.T.astype(BF16).reshape(2, 192, D)
        for s in range(8):
            grad[l, s, pl.ds(576, 16), :] = small[l].astype(BF16)
        pltpu.make_async_copy(grad.at[l], g_all.at[l], gsem.at[l]).start()
    for l in (1, 0):
        pltpu.make_async_copy(grad.at[l], g_all.at[l], gsem.at[l]).wait()


def compute(count, img, cot, w_all, sp):
    V = pl.BlockSpec(memory_space=pltpu.VMEM)
    A = pl.BlockSpec(memory_space=pl.ANY)
    vm = pltpu.VMEM
    return pl.pallas_call(
        compute_kernel,
        out_shape=(
            jax.ShapeDtypeStruct((NI, SEQ, D), F32),
            jax.ShapeDtypeStruct((NI, SEQ, D), F32),
            jax.ShapeDtypeStruct((2, 8, BLK, D), BF16),
        ),
        in_specs=[pl.BlockSpec(memory_space=pltpu.SMEM), V, V, A, V],
        out_specs=(V, V, A),
        scratch_shapes=[
            vm((2, 8, 48, 3 * D), BF16), vm((2, 8, 48, D), BF16), vm((2, 8, 48, FF), BF16),
            vm((2, 8, 192, D), BF16),
            vm((2, T, D), F32), vm((2, T, D), F32),
            vm((2, T, D), BF16), vm((2, T, D), BF16), vm((2, T, D), BF16),
            vm((2, T, 3 * D), BF16), vm((2, T, FF), BF16), vm((2, T, FF), BF16),
            vm((T, D), F32), vm((T, D), BF16), vm((T, D), BF16), vm((T, D), BF16),
            vm((2, NI, 8, R), F32),
            vm((2, 8, BLK, D), BF16), vm((2, 16, D), F32),
            pltpu.SemaphoreType.DMA((2, 9)), pltpu.SemaphoreType.DMA((2,)),
        ],
        compiler_params=pltpu.CompilerParams(vmem_limit_bytes=63 * 1024 * 1024),
        cost_estimate=pl.CostEstimate(flops=28_000_000_000, bytes_accessed=20_000_000, transcendentals=8_000_000),
    )(count, img, cot, w_all, sp)


PZ = 80
MESH = pl.DeviceIdType.MESH


def place():
    r = lax.axis_index("replica")
    s = lax.axis_index("shard")
    core = lax.rem(r, 2)
    xlo = lax.rem(lax.div(r, 2), 2)
    return dict(x=lax.rem(s, 2) * 2 + xlo, y=lax.div(s, 2), z=lax.div(r, 4), c=core)


def device(p, **change):
    q = dict(p, **change)
    return (q["z"] * 4 + lax.rem(q["x"], 2) * 2 + q["c"], q["y"] * 2 + lax.div(q["x"], 2))


def step_on(p, axis, d):
    return lax.rem(p[axis] + d, 4)


def part(ref, t, x=None, y=None, z=None):
    w = slice(None)
    return ref.at[w if y is None else y, w if x is None else lax.div(x, 2),
                  w if x is None else lax.rem(x, 2), w if z is None else z,
                  :, pl.ds(128 * t, 128)]


class Sender:
    def __init__(self, send, recv):
        self.send, self.recv, self.n, self.out = send, recv, 0, []

    def __call__(self, src, dst, dev):
        cp = pltpu.make_async_remote_copy(src_ref=src, dst_ref=dst, send_sem=self.send.at[self.n],
                                          recv_sem=self.recv.at[self.n], device_id=dev,
                                          device_id_type=MESH)
        self.n += 1
        cp.start()
        self.out.append(cp)
        return cp

    def drain(self):
        for cp in self.out:
            cp.wait_send()


def greet(devs):
    barrier = pltpu.get_barrier_semaphore()
    for dev in devs:
        pl.semaphore_signal(barrier, inc=1, device_id=dev, device_id_type=MESH)
    pl.semaphore_wait(barrier, len(devs))


def fetch_kernel(joint, merge, expand, reduce_w, vec, w, own, send, recv, lsem):
    p = place()
    c, x, y, z = p["c"], p["x"], p["y"], p["z"]
    xhi, xlo = lax.div(x, 2), lax.rem(x, 2)
    partner = device(p, c=1 - c)
    across = device(p, x=3 - x)
    devs = [partner] + [device(p, **{a: step_on(p, a, d)}) for a in "xyz" for d in (1, 2, 3)]
    barrier = pltpu.get_barrier_semaphore()
    for dev in devs:
        pl.semaphore_signal(barrier, inc=1, device_id=dev, device_id_type=MESH)

    blocks = []
    for cb in range(3):
        blocks.append((48 * cb, joint[c, :, pl.ds(D * cb, D)]))
    blocks.append((144, merge[c]))
    for cb in range(4):
        blocks.append((192 + 48 * cb, expand[c, :, pl.ds(D * cb, D)]))
    blocks.append((384, reduce_w[c]))
    blocks.append((576, vec[c]))
    flat = jnp.concatenate([b.astype(BF16) for _, b in blocks]
                           + [jnp.zeros((48, D), BF16)], axis=0)
    own[...] = flat.reshape(2, 4, PZ, D)
    pl.semaphore_wait(barrier, len(devs))

    go = Sender(send, recv)
    wc = w.at[c]

    def mine(t, a=None, b=None):
        s = slice(None)
        return own.at[s if a is None else a, s if b is None else b, :, pl.ds(128 * t, 128)]

    def home(t, a=None, b=None):
        s = slice(None)
        return wc.at[y, xhi, s if a is None else a, s if b is None else b, :, pl.ds(128 * t, 128)]

    local = []
    for t, (a, b) in enumerate([(xlo, None), (None, z), (None, None)]):
        cp = pltpu.make_async_copy(mine(t, a, b), home(t, a, b), lsem.at[t])
        cp.start()
        local.append(cp)
    c1 = go(mine(2), home(2), across)
    a1 = [go(mine(0, xlo, None), home(0, xlo, None), device(p, y=step_on(p, "y", d))) for d in (1, 3, 2)]
    b1 = [go(mine(1, None, z), home(1, None, z), device(p, y=step_on(p, "y", d))) for d in (1, 3, 2)]
    for cp in local:
        cp.wait()
    c1.wait_recv()
    src = part(wc, 2, y=y)
    c2 = [go(src, src, device(p, y=step_on(p, "y", d))) for d in (1, 3, 2)]
    for cp in a1:
        cp.wait_recv()
    src = part(wc, 0, x=x)
    a2 = [go(src, src, device(p, x=step_on(p, "x", d))) for d in (1, 3, 2)]
    for cp in b1:
        cp.wait_recv()
    src = wc.at[:, xhi, :, z, :, pl.ds(128, 128)]
    b2 = go(src, src, across)
    b2.wait_recv()
    src = part(wc, 1, z=z)
    b3 = [go(src, src, device(p, z=step_on(p, "z", d))) for d in (1, 3, 2)]
    last = []
    fw = lambda r: last.append(go(r, r, partner))
    fw(part(wc, 0, x=x))
    fw(part(wc, 1, z=z))
    fw(part(wc, 2, y=y))
    for k, d in enumerate((3, 1, 2)):
        a2[k].wait_recv()
        fw(part(wc, 0, x=step_on(p, "x", d)))
        c2[k].wait_recv()
        fw(part(wc, 2, y=step_on(p, "y", d)))
        b3[k].wait_recv()
        fw(part(wc, 1, z=step_on(p, "z", d)))
    for cp in last:
        cp.wait_recv()
    go.drain()


def fetch(joint, merge, expand, reduce_w, vec):
    V = pl.BlockSpec(memory_space=pltpu.VMEM)
    return pl.pallas_call(
        fetch_kernel,
        out_shape=jax.ShapeDtypeStruct((2, 4, 2, 2, 4, PZ, D), BF16),
        in_specs=[V] * 5,
        out_specs=pl.BlockSpec(memory_space=pl.ANY),
        scratch_shapes=[pltpu.VMEM((2, 4, PZ, D), BF16), pltpu.SemaphoreType.DMA((32,)),
                        pltpu.SemaphoreType.DMA((32,)), pltpu.SemaphoreType.DMA((3,))],
        compiler_params=pltpu.CompilerParams(collective_id=0, has_side_effects=True,
                                             vmem_limit_bytes=32 * 1024 * 1024),
    )(joint, merge, expand, reduce_w, vec)


ORDER = ("xyz", "yzx", "zxy")


def reduce_kernel(g, o, s_buf, cr, ra1, rb1, rc1, ra2, rb2, rc2, ra3, rb3, rc3, o_buf,
                  send, recv, lsem):
    p = place()
    c, x, y, z = p["c"], p["x"], p["y"], p["z"]
    xhi, xlo = lax.div(x, 2), lax.rem(x, 2)
    partner = device(p, c=1 - c)
    devs = [partner] + [device(p, **{a: step_on(p, a, d)}) for a in "xyz" for d in (1, 2, 3)]
    xpair = xhi * 2 + 1 - xlo
    devs += [device(p, x=xpair, z=step_on(p, "z", d)) for d in (1, 2, 3)]
    greet(devs)
    go = Sender(send, recv)
    slots = [[ra1, ra2, ra3], [rb1, rb2, rb3], [rc1, rc2, rc3]]

    swaps, loads = {}, {}
    for n, d in enumerate((1, 3, 2, 0)):
        for t in range(3):
            a = ORDER[t][0]
            at = {a: step_on(p, a, d)}
            swaps[t, d] = go(part(g.at[1 - c], t, **at), part(cr, t, **at), partner)
            cp = pltpu.make_async_copy(part(g.at[c], t, **at), part(s_buf, t, **at),
                                       lsem.at[3 * n + t])
            cp.start()
            loads[t, d] = cp

    def each(t, fixed, body):
        free = [a for a in "yxz" if a not in fixed]
        n = 4 ** len(free)

        def one(i, _):
            at = dict(fixed)
            k = i
            for a in reversed(free):
                at[a] = lax.rem(k, 4)
                k = lax.div(k, 4)
            body(at, free)
            return 0

        if n == 1:
            one(0, 0)
        else:
            lax.fori_loop(0, n, one, 0)

    def spot(at, t):
        return (at["y"], lax.div(at["x"], 2), lax.rem(at["x"], 2), at["z"], slice(None),
                pl.ds(128 * t, 128))

    def slot_index(d, at, free):
        idx = [d - 1]
        for a in free:
            idx += [lax.div(at["x"], 2), lax.rem(at["x"], 2)] if a == "x" else [at[a]]
        return tuple(idx)

    first = {}
    for d in (1, 3, 2, 0):
        for t in range(3):
            a = ORDER[t][0]
            pos = step_on(p, a, d)
            loads[t, d].wait()
            swaps[t, d].wait_recv()

            def merge(at, free, t=t):
                k = spot(at, t)
                s_buf[k] = (s_buf[k].astype(F32) + cr[k].astype(F32)).astype(BF16)

            each(t, {a: pos}, merge)
            if d:
                first[t, d] = go(part(s_buf, t, **{a: pos}), slots[t][0].at[d - 1],
                                 device(p, **{a: pos}))
    held = [dict(), dict(), dict()]
    waiting = first
    for stage in range(3):
        nxt = {}
        for t in range(3):
            a = ORDER[t][stage]
            held[t][a] = p[a]
            for d in (1, 3, 2):
                waiting[t, d].wait_recv()

            def add(at, free, t=t, stage=stage):
                k = spot(at, t)
                v = s_buf[k].astype(F32)
                for d in (1, 2, 3):
                    v = v + slots[t][stage][slot_index(d, at, free)].astype(F32)
                s_buf[k] = v.astype(BF16)

            each(t, held[t], add)
            if stage < 2:
                b = ORDER[t][stage + 1]
                for d in (1, 3, 2):
                    pos = step_on(p, b, d)
                    nxt[t, d] = go(part(s_buf, t, **dict(held[t], **{b: pos})),
                                   slots[t][stage + 1].at[d - 1], device(p, **{b: pos}))
        waiting = nxt

    mine = s_buf.at[y, xhi, xlo, z]
    keep = pltpu.make_async_copy(mine, o_buf.at[c, xlo, z], lsem.at[12])
    keep.start()
    out = []
    for xx in (xpair, x):
        for d in (1, 3, 2, 0):
            if d == 0 and xx is x:
                continue
            out.append(go(mine, o_buf.at[c, xlo, z], device(p, x=xx, z=step_on(p, "z", d))))
    keep.wait()
    for cp in out:
        cp.wait_recv()
    final = go(o_buf.at[c], o_buf.at[c], partner)
    final.wait_recv()
    cp = pltpu.make_async_copy(o_buf, o, lsem.at[13])
    cp.start()
    go.drain()
    cp.wait()


def reduce_grads(g):
    A = pl.BlockSpec(memory_space=pl.ANY)
    vm = lambda *shape: pltpu.VMEM(shape, BF16)
    return pl.pallas_call(
        reduce_kernel,
        out_shape=jax.ShapeDtypeStruct((2, 2, 4, PZ, D), BF16),
        in_specs=[A],
        out_specs=A,
        scratch_shapes=[
            vm(4, 2, 2, 4, PZ, D), vm(4, 2, 2, 4, PZ, D),
            vm(3, 4, 4, PZ, 128), vm(3, 2, 2, 4, PZ, 128), vm(3, 4, 2, 2, PZ, 128),
            vm(3, 4, PZ, 128), vm(3, 2, 2, PZ, 128), vm(3, 4, PZ, 128),
            vm(3, PZ, 128), vm(3, PZ, 128), vm(3, PZ, 128),
            vm(2, 2, 4, PZ, D),
            pltpu.SemaphoreType.DMA((48,)), pltpu.SemaphoreType.DMA((48,)),
            pltpu.SemaphoreType.DMA((14,)),
        ],
        compiler_params=pltpu.CompilerParams(collective_id=1, has_side_effects=True,
                                             vmem_limit_bytes=48 * 1024 * 1024),
    )(g)


BETA_ONE = 0.9
BETA_TWO = 0.999
ADAM_EPS = 1e-08
DECAY_MATRIX = 0.05
RATE_MATRIX = 0.05
RATE_SMALL = 0.4
STEP = 10


def adam_update(gradient, first_moment, second_moment, master, step_rate, decay_rate):
    first_new = BETA_ONE * first_moment + (1.0 - BETA_ONE) * gradient
    second_new = BETA_TWO * second_moment + (1.0 - BETA_TWO) * gradient * gradient
    corrected = first_new / (1.0 - BETA_ONE**STEP)
    denominator = jnp.sqrt(second_new / (1.0 - BETA_TWO**STEP)) + ADAM_EPS
    master_new = master - step_rate * (corrected / denominator + decay_rate * master)
    return (first_new, second_new, master_new)


def adam_kernel(g, *refs):
    ins, outs = refs[:12], refs[12:]
    i = pl.program_id(1)
    for kind, (at, blocks, rows) in enumerate([(0, 3, 16), (144, 1, 16), (192, 4, 16), (384, 1, 64)]):
        step = 48 if rows == 16 else 192
        for cb in range(blocks):
            start = pl.multiple_of(at + step * cb + i * rows, 16)
            grad = g[0, pl.ds(start, rows), :].astype(F32)
            cols = (0, slice(None), pl.ds(D * cb, D))
            m, v, w = (ins[3 * kind + k][cols] for k in range(3))
            new = adam_update(grad, m, v, w, RATE_MATRIX, DECAY_MATRIX)
            for k, val in enumerate((grad,) + new):
                outs[4 * kind + k][cols] = val


def adam(g, firsts, seconds, masters):
    widths = (3 * D, D, 4 * D, D)
    rows = (16, 16, 16, 64)
    spec = [pl.BlockSpec((1, r, w), lambda l, i: (l, i, 0)) for r, w in zip(rows, widths)]
    ins, in_specs, out_specs, shapes = [], [], [], []
    for k in range(4):
        for a in (firsts[k], seconds[k], masters[k]):
            ins.append(a)
            in_specs.append(spec[k])
        for _ in range(4):
            out_specs.append(spec[k])
            shapes.append(jax.ShapeDtypeStruct(masters[k].shape, F32))
    return pl.pallas_call(
        adam_kernel,
        grid=(2, 3),
        out_shape=tuple(shapes),
        in_specs=[pl.BlockSpec((1, BLK, D), lambda l, i: (l, 0, 0))] + in_specs,
        out_specs=tuple(out_specs),
    )(g, *ins)


def shards(images, cotangent, image_count, joint_weight, merge_weight, expand_weight,
           reduce_weight, small_params, joint_first, merge_first, expand_first, reduce_first,
           small_first, joint_second, merge_second, expand_second, reduce_second, small_second):
    masters = (joint_weight, merge_weight, expand_weight, reduce_weight)
    firsts = (joint_first, merge_first, expand_first, reduce_first)
    seconds = (joint_second, merge_second, expand_second, reduce_second)
    width = small_params.shape[1]
    vec = jnp.pad(small_params, ((0, 0), (0, 16 * D - width))).reshape(2, 16, D)
    w = fetch(*masters, vec).reshape(2, 8, BLK, D)
    sp = w[:, :, 576:578].reshape(2, 8, 2 * D)[:, :, :width].reshape(2, 9, D).astype(F32)
    sp = jnp.pad(sp, ((0, 0), (0, 7), (0, 0)))
    block_out, image_grad, g = compute(image_count, images, cotangent, w, sp)
    total = reduce_grads(g.reshape(2, 4, 2, 2, 4, PZ, D)).reshape(2, BLK, D)
    done = adam(total, firsts, seconds, masters)
    rank = lax.axis_index("shard")
    vec_grad = lax.dynamic_slice_in_dim(total[:, 576:585].reshape(2, 9 * D), rank * width, width, 1)
    vec_grad = vec_grad.astype(F32)
    vec_done = (vec_grad,) + adam_update(vec_grad, small_first, small_second, small_params,
                                         RATE_SMALL, 0.0)
    outputs = [block_out, image_grad]
    for member in range(4):
        outputs += [done[4 * kind + member] for kind in range(4)] + [vec_done[member]]
    return tuple(outputs)


def solution(mesh):
    whole = P(("replica", "shard"), None, None)
    weights = [P(None, "shard", None)] * 4 + [P(None, "shard")]
    return jax.shard_map(
        shards,
        mesh=mesh,
        in_specs=(whole, whole, P(("replica", "shard"))) + tuple(weights * 3),
        out_specs=(whole, whole) + tuple(weights * 4),
        check_vma=False,
    )
```

time: 695 us -> 229 us (0.33)
  waiting for transfers between devices: 225 us -> 0 us
  Pallas kernels: 0 us -> 216 us
  matrix products: 130 us -> 0 us
  local copies, waits for them, and re-layouts: 124 us -> 9.67 us
  blocking collectives: 110 us -> 0 us
  other arithmetic: 84.7 us -> 1.34 us
  between operations: 16 us -> 1.45 us
    pallas_call x0 -> x4, Pallas kernels: none -> 216 us  [the longest x1 113 us: compute(): pl.pallas_call(compute_kernel, out_shape=(jax.ShapeDtypeStruct((NI, SEQ,...]
    unnamed x6 -> x0, waiting for transfers between devices: 166 us -> none
    dot_general x36 -> x0, matrix products: 130 us -> none  [the longest x2 13.3 us: backward_layer(): jnp.einsum('isd,fd->isf', branch_grad, reduce_w, preferred_element_type=j...]
    unnamed x1 -> x0, blocking collectives: 64.9 us -> none
    all_gather x4 -> x0, waiting for transfers between devices: 58.8 us -> none  [the longest x3 48.7 us: side_by_side(): lax.all_gather(both, axis, axis=dim, tiled=True)]
    convert_element_type x11 -> x0, other arithmetic: 45.3 us -> none  [the longest x2 35.6 us: forward_layer(): active = exact_gelu(hidden).astype(jnp.bfloat16)]
    all_gather x2 -> x0, blocking collectives: 45 us -> none  [the longest x1 26.7 us: shards(): lax.all_gather(low_copy[4], 'shard', axis=1, tiled=True)]
    another operation x10 -> x0, local copies, waits for them, and re-layouts: 30.5 us -> none  [the longest x8 24.5 us: shards(): jnp.stack([layer_terms[layer_index][kind_index] for layer_index in range(...]
  transfers between devices with their start and end apart: 5 -> 0, of which waited for: 3 -> 0; matrix products, arithmetic and copies ran while one was open for 12% -> 0% of each run, Pallas kernels for 0% -> 0%
where the time goes in v1:
time: 229 us; the launch traced here: 228 us
  Pallas kernels  216 us (94%)
  local copies, waits for them, and re-layouts  9.67 us (4%)
    pallas_call x1, Pallas kernels, compute(): pl.pallas_call(compute_kernel, out_shape=(jax.ShapeDtypeStruct((NI, SEQ,...  113 us
    pallas_call x1, Pallas kernels, fetch(): pl.pallas_call(fetch_kernel, out_shape=jax.ShapeDtypeStruct((2, 4, 2, 2,...  47.8 us
    pallas_call x1, Pallas kernels, reduce_grads(): pl.pallas_call(reduce_kernel, out_shape=jax.ShapeDtypeStruct((2, 2, 4, PZ...  46.8 us
    unnamed x21, local copies, waits for them, and re-layouts  8.82 us
    pallas_call x1, Pallas kernels, adam(): pl.pallas_call(adam_kernel, grid=(2, 3), out_shape=tuple(shapes), in_spec...  7.46 us

profile of v1, /device:TPU:1, one launch (start us, length us, event | category | flops | bytes accessed | tf_op | source)
XLA Modules:
  0.0 228.0 jit_solution(2357957803457923915)
XLA Ops:
  0.7 0.7 pad.10
  1.4 0.0 copy-start.2
  1.4 1.1 copy-done.2
  2.4 0.0 copy-start.3
  2.4 1.1 copy-done.3
  3.5 0.0 copy-start.4
  3.5 1.0 copy-done.4
  4.5 0.0 copy-start.5
  4.5 0.9 copy-done.5
  5.4 47.8 %shard_map.345 = bf16[2,4,2,2,4,80,384]{6,5,4,3,2,1,0:T(8,128)(2,1)S(1)} custom-call(f32[2,48,1152]{2,1,0:T(8,128)S(1)} %copy-done.4, f32[2,48,384]{2,1,0:T(8,128)S(1)} %copy-done.5, f32[2,48,1536]{2,1,0:T(8,128)S(1)} %copy-done.2, f32[2,192,384]{2,1,0:T(8,128)S(1)} %copy-done.3, f32[2,16,384]{2,1,0:T(8,128)S(1)} %bitcast.14), custom_call_target="tpu_custom_call" | custom-call | tf_op jit(solution)/shard_map/pallas_call | solution.py:440
  53.2 0.0 copy-start
  53.2 3.0 %copy-done = bf16[2,4,2,2,4,80,384]{6,5,4,3,2,1,0:T(8,128)(2,1)} copy-done((bf16[2,4,2,2,4,80,384]{6,5,4,3,2,1,0:T(8,128)(2,1)}, bf16[2,4,2,2,4,80,384]{6,5,4,3,2,1,0:T(8,128)(2,1)S(1)}, u32[]{:S(2)}) %copy-start) | copy-done | bytes 7864344
  56.3 0.1 convert_element_type.11
  56.4 0.6 pad_convert_fusion.sp
  57.7 113.5 %shard_map.346 = (f32[6,197,384]{2,1,0:T(8,128)}, f32[6,197,384]{2,1,0:T(8,128)}, bf16[2,8,640,384]{3,2,1,0:T(8,128)(2,1)}) custom-call(s32[1]{0:T(128)S(6)} %copy.44.count, bf16[6,197,384]{2,1,0:T(8,128)(2,1)} %img.1, bf16[6,197,384]{2,1,0:T(8,128)(2,1)} %cot.1, bf16[2,8,640,384]{3,2,1,0:T(8,128)(2,1)} %bitcast.11, f32[2,16,384]{2,1,0:T(8,128)} %pad_convert_fusion.sp), custom_call_target="tpu_custom_call" | custom-call | flops 28000000000 | bytes 20000000 | tf_op jit(solution)/shard_map/pallas_call | solution.py:284
  171.2 0.0 copy-start.6
  171.2 0.0 copy-start.7
  171.2 0.0 copy-start.8
  171.3 46.8 %shard_map.347 = bf16[2,2,4,80,384]{4,3,2,1,0:T(8,128)(2,1)S(1)} custom-call(bf16[2,4,2,2,4,80,384]{6,5,4,3,2,1,0:T(8,128)(2,1)} %bitcast.15), custom_call_target="tpu_custom_call" | custom-call | tf_op jit(solution)/shard_map/pallas_call | solution.py:572
  218.1 0.0 copy-start.1
  218.1 0.9 copy-done.1
  219.0 7.5 %shard_map.348 = (f32[2,48,1152]{2,1,0:T(8,128)}, f32[2,48,1152]{2,1,0:T(8,128)}, f32[2,48,1152]{2,1,0:T(8,128)}, f32[2,48,1152]{2,1,0:T(8,128)}, f32[2,48,384]{...) custom-call(bf16[2,640,384]{2,1,0:T(8,128)(2,1)} %bitcast.12, ...), custom_call_target="tpu_custom_call" | custom-call | tf_op jit(solution)/shard_map/pallas_call | solution.py:636
  226.5 0.7 slice_bitcast_fusion
  227.2 0.0 copy-done.6
  227.3 0.0 copy-done.7
  227.3 0.0 copy-done.8
  227.3 0.7 multiply_subtract_fusion
  (5 shorter events, 0.1 us)
Async XLA Ops:
  1.4 1.1 copy-start.2
  2.4 1.1 copy-start.3
  3.5 1.0 copy-start.4
  4.5 0.9 copy-start.5
  53.2 3.1 %copy-start = (bf16[2,4,2,2,4,80,384]{6,5,4,3,2,1,0:T(8,128)(2,1)}, bf16[2,4,2,2,4,80,384]{6,5,4,3,2,1,0:T(8,128)(2,1)S(1)}, u32[]{:S(2)}) copy-start(bf16[2,4,2,2,4,80,384]{6,5,4,3,2,1,0:T(8,128)(2,1)S(1)} %shard_map.345) | copy-start | bytes 23592964
  171.2 56.0 %copy-start.6 = (f32[2,432]{1,0:T(2,128)S(1)}, f32[2,432]{1,0:T(2,128)}, u32[]{:S(2)}) copy-start(f32[2,432]{1,0:T(2,128)} %param.25) | copy-start | bytes 10372
  171.2 56.0 %copy-start.7 = (f32[2,432]{1,0:T(2,128)S(1)}, f32[2,432]{1,0:T(2,128)}, u32[]{:S(2)}) copy-start(f32[2,432]{1,0:T(2,128)} %param.35) | copy-start | bytes 10372
  171.2 56.0 %copy-start.8 = (f32[2,432]{1,0:T(2,128)S(1)}, f32[2,432]{1,0:T(2,128)}, u32[]{:S(2)}) copy-start(f32[2,432]{1,0:T(2,128)} %param.30) | copy-start | bytes 10372
  218.1 0.9 copy-start.1
